TPU v7x, 32 devices: a whole 2x2x4 slice. The times are simulated.
32 devices in a mesh: prow: 8 (over z, x), pcol: 4 (over y, core).
Axes of the slice: x: 2, y: 2, z: 4, core: 2. Of those that a mesh axis runs over, the one named last changes fastest.
Arguments:
- sigma_top: bfloat16 [8192, 8192], P('prow', 'pcol'), may hold values from -400 to 400, as said below
- panel_par: bfloat16 [8192, 1024], P('prow', 'pcol'), may hold values from -0.119628906 to 0.119628906
- panel_kid: bfloat16 [8192, 2048], P('prow', 'pcol'), may hold values from -0.119628906 to 0.119628906
- link_kid: bfloat16 [8, 256, 256], P('pcol'), may hold values from -0.23925781 to 0.23925781
- dinv_par: float32 [4, 256, 256], P('pcol'), may hold values from -6 to 6
- dinv_kid: float32 [8, 256, 256], P('pcol'), may hold values from -6 to 6
- mask_par: int32 [4, 32], P('pcol', 'prow'), may hold values 0 or 1
- mask_kid: int32 [8, 32], P('pcol', 'prow'), may hold values 0 or 1
Outputs:
- sigma_par: bfloat16 [8192, 1024], P('prow', 'pcol')
- diag_par: float32 [4, 256, 256], P('pcol')
- sigma_kid: bfloat16 [8192, 2048], P('prow', 'pcol')
- link_sigma: float32 [8, 256, 256], P('pcol')
- diag_kid: float32 [8, 256, 256], P('pcol')
Inputs may be any that keep to these rules, and one draw needn't show every extreme that they name: `sigma_top`: symmetric.
All inputs are finite; a program needn't handle non-finite values. No bound on the sum of `mask_par` or of `mask_kid` on one device may be relied on, other than what follows from the above.
Results may differ from a plain program's by a relative error of at most 0.015.
Values may be sent and summed in bfloat16 or wider, within the bound.
A program may use at most 64 MiB of HBM per device.

v0:
```python
import jax
import jax.numpy as jnp
from jax import lax
from jax.sharding import PartitionSpec as P

KIDS = 2


def expand_rows(mask, width):
    count, blocks = mask.shape
    spread = jnp.broadcast_to(
        mask.T.astype(jnp.float32)[:, None, :, None], (blocks, width, count, width)
    )
    return spread.reshape(blocks * width, count * width)


def batch_mult(left, right):
    return jnp.einsum("cab,cbd->cad", left, right, precision=lax.Precision.HIGHEST)


def batch_tmult(left, right):
    return jnp.einsum("cba,cbd->cad", left, right, precision=lax.Precision.HIGHEST)


def on_device(sigma_top, panel_par, panel_kid, link_kid, dinv_par, dinv_kid, mask_par, mask_kid):
    width = dinv_par.shape[1]
    par_here = dinv_par.shape[0]
    kid_here = dinv_kid.shape[0]
    row_count = sigma_top.shape[0]
    kid_pattern = mask_kid * jnp.repeat(mask_par, KIDS, axis=0)
    par_rows = expand_rows(mask_par, width)
    kid_rows = expand_rows(kid_pattern, width)
    low_par = panel_par * par_rows.astype(jnp.bfloat16)
    low_kid = panel_kid * kid_rows.astype(jnp.bfloat16)
    sigma_rows = lax.all_gather(sigma_top, "pcol", axis=1, tiled=True)
    prod_par = jnp.dot(
        sigma_rows,
        lax.all_gather(low_par, "prow", axis=0, tiled=True),
        preferred_element_type=jnp.float32,
    )
    prod_kid = jnp.dot(
        sigma_rows,
        lax.all_gather(low_kid, "prow", axis=0, tiled=True),
        preferred_element_type=jnp.float32,
    )
    sigma_par = (-prod_par * par_rows).astype(jnp.bfloat16)
    par_blocks = sigma_par.reshape(row_count, par_here, width)
    par_spread = jnp.repeat(par_blocks, KIDS, axis=1)
    carried = jnp.einsum("rcb,cbd->rcd", par_spread, link_kid, preferred_element_type=jnp.float32)
    sigma_kid = (-(prod_kid + carried.reshape(row_count, kid_here * width)) * kid_rows).astype(
        jnp.bfloat16
    )
    low_par3 = low_par.reshape(row_count, par_here, width)
    low_kid3 = low_kid.reshape(row_count, kid_here, width)
    kid_blocks = sigma_kid.reshape(row_count, kid_here, width)
    part_par = jnp.einsum("rpb,rpd->pbd", low_par3, par_blocks, preferred_element_type=jnp.float32)
    part_cross = jnp.einsum(
        "rcb,rcd->cbd", par_spread, low_kid3, preferred_element_type=jnp.float32
    )
    part_kid = jnp.einsum("rcb,rcd->cbd", low_kid3, kid_blocks, preferred_element_type=jnp.float32)
    link_wide = link_kid.astype(jnp.float32)
    sum_par = lax.psum(part_par.astype(jnp.bfloat16), "prow").astype(jnp.float32)
    diag_par = dinv_par - sum_par
    diag_spread = jnp.repeat(diag_par, KIDS, axis=0)
    cross_sum, kid_sum = (
        lax.psum(part_cross.astype(jnp.bfloat16), "prow").astype(jnp.float32),
        lax.psum(part_kid.astype(jnp.bfloat16), "prow").astype(jnp.float32),
    )
    link_sigma = -(cross_sum + batch_mult(diag_spread, link_wide))
    diag_kid = dinv_kid - kid_sum - batch_tmult(link_wide, link_sigma)
    return (sigma_par, diag_par, sigma_kid, link_sigma, diag_kid)


def solution(mesh):
    placed = (
        P("prow", "pcol"),
        P("prow", "pcol"),
        P("prow", "pcol"),
        P("pcol", None, None),
        P("pcol", None, None),
        P("pcol", None, None),
        P("pcol", "prow"),
        P("pcol", "prow"),
    )
    return jax.shard_map(
        on_device,
        mesh=mesh,
        in_specs=placed,
        out_specs=(
            P("prow", "pcol"),
            P("pcol", None, None),
            P("prow", "pcol"),
            P("pcol", None, None),
            P("pcol", None, None),
        ),
        check_vma=False,
    )
```

profile of v0, /device:TPU:0, one launch (start us, length us, event | category | flops | bytes accessed | tf_op | source)
XLA Modules:
  0.0 421.5 jit_solution(7698292222596817835)
XLA Ops:
  7.2 0.0 copy-start
  7.2 0.0 copy-start.11
  7.2 0.0 copy-start.6
  7.2 0.0 copy-start.10
  7.2 0.0 all-gather.4.cloned.1.call-start
  7.3 0.7 bitcast_convert_fusion
  8.0 0.1 broadcast_bitcast_fusion
  8.1 2.0 broadcast_multiply_fusion
  10.1 0.0 all-gather.4.cloned.1.call-update
  10.2 0.0 all-gather.6.cloned.1.call-start
  10.2 0.7 all-gather.6.cloned.1.call-update
  10.9 0.0 all-gather.8.cloned.1.call-start
  11.0 0.0 copy-done.6
  11.0 1.3 copy.13
  12.3 0.0 copy-done.11
  12.3 0.0 copy-done.10
  12.3 0.3 broadcast_in_dim.25
  12.6 0.5 copy.29
  13.1 0.4 copy-done.3
  13.5 1.2 convert_multiply_fusion
  14.7 0.0 all-gather.8.cloned.1.call-update
  14.7 0.0 copy-start.1
  14.8 0.0 all-reduce.3.cloned.1.call-start
  14.8 72.1 %all-gather.4.cloned.1.call-done = bf16[8192,256]{1,0:T(8,128)(2,1)} async-done(((bf16[1024,256]{1,0:T(8,128)(2,1)}), bf16[8192,256]{1,0:T(8,128)(2,1)}) %all-gather.4.cloned.1.call-update) | async-done | bytes 4194320 | tf_op jit(solution)/shard_map/all_gather | solution.py:38
  86.9 105.8 %all-gather.6.cloned.1.call-done = bf16[1024,8192]{1,0:T(8,128)(2,1)} async-done(((bf16[1024,2048]{1,0:T(8,128)(2,1)}), bf16[1024,8192]{1,0:T(8,128)(2,1)}) %all-gather.6.cloned.1.call-update) | async-done | bytes 16777232 | tf_op jit(solution)/shard_map/all_gather | solution.py:35
  192.7 11.6 %fusion.4 = bf16[256,1024]{1,0:T(8,128)(2,1)S(1)} fusion(bf16[8192,256]{1,0:T(8,128)(2,1)} %all-gather.4.cloned.1.call-done, bf16[1024,8192]{1,0:T(8,128)(2,1)} %all-gather.6.cloned.1.call-done, f32[1024]{0:T(1024)S(1)} %bitcast.58), kind=kOutput, calls=%fused_computation.6 | convolution fusion | flops 4295753728 | bytes 21499904 | tf_op jit(solution)/shard_map/dot_general | solution.py:36
  204.3 0.0 copy-done.1
  204.3 1.0 fusion.7
  205.3 2.4 convolution_convert_fusion.1
  207.7 0.0 copy-done
  207.7 1.9 fusion.9
  209.6 110.7 %all-gather.8.cloned.1.call-done = bf16[8192,512]{0,1:T(8,128)(2,1)} async-done(((bf16[1024,512]{0,1:T(8,128)(2,1)}), bf16[8192,512]{0,1:T(8,128)(2,1)}) %all-gather.8.cloned.1.call-update) | async-done | bytes 8388624 | tf_op jit(solution)/shard_map/all_gather | solution.py:43
  320.4 15.2 %fusion.2 = bf16[1024,512]{0,1:T(8,128)(2,1)S(1)} fusion(f32[1024,512]{0,1:T(8,128)S(1)} %bitcast.48, f32[2,1024,256]{1,2,0:T(8,128)} %fusion.9, bf16[8192,512]{0,1:T(8,128)(2,1)} %all-gather.8.cloned.1.call-done, bf16[1024,8192]{1,0:T(8,128)(2,1)} %all-gather.6.cloned.1.call-done), kind=kOutput, calls=%fused_computation.3 | convolution fusion | flops 8592031744 | bytes 30408704 | tf_op jit(solution)/shard_map/dot_general | solution.py:41
  335.6 0.0 copy-start.9
  335.6 0.0 copy-start.8
  335.7 1.0 copy-done.7
  336.6 1.2 convolution_convert_fusion
  337.8 0.0 all-reduce.3.cloned.1.call-update
  337.8 1.0 copy.20
  338.8 2.3 copy.21
  341.1 69.0 %all-reduce.3.cloned.1.call-done = (bf16[1,256,256]{2,1,0:T(8,128)(2,1)}, bf16[2,256,256]{2,1,0:T(8,128)(2,1)}, bf16[2,256,256]{2,1,0:T(8,128)(2,1)}) async-done(((bf16[1,256,256]{2,1,0:T(8,128)(2,1)}, bf16[2,256,256]{2,1,0:T(8,128)(2,1)}, bf16[2,256,256]{2,1,0:T(8,128)(2,1)}), (bf16[1,256,256]{2,1,0:T(8,128)(2,1)}, bf16[2,256,256]{2,1,0:T(8,128)(2,1)}, ...) | async-done | bytes 655376 | tf_op jit(solution)/shard_map/psum | solution.py:62
  410.1 0.0 copy-done.9
  410.1 0.9 convert_subtract_fusion
  411.1 0.0 copy-start.5
  411.1 1.5 fusion.6
  412.5 0.0 copy-start.4
  412.6 0.0 copy-done.8
  412.6 2.4 fusion.5
  (9 shorter events, 0.0 us)
Async XLA Ops:
  7.2 200.6 %copy-start = (bf16[2,256,256]{2,1,0:T(8,128)(2,1)S(1)}, bf16[2,256,256]{2,1,0:T(8,128)(2,1)}, u32[]{:S(2)}) copy-start(bf16[2,256,256]{2,1,0:T(8,128)(2,1)} %param.11) | copy-start | bytes 786436
  7.2 5.1 %copy-start.11 = (s32[1,4]{1,0:T(1,128)S(1)}, s32[1,4]{1,0:T(1,128)}, u32[]{:S(2)}) copy-start(s32[1,4]{1,0:T(1,128)} %param.14) | copy-start | bytes 52
  7.2 3.8 copy-start.6
  7.2 5.1 %copy-start.10 = (s32[2,4]{1,0:T(2,128)S(1)}, s32[2,4]{1,0:T(2,128)}, u32[]{:S(2)}) copy-start(s32[2,4]{1,0:T(2,128)} %param.15) | copy-start | bytes 100
  7.2 79.7 %all-gather.4.cloned.1.call-start = ((), (), s32[]{:S(2)}) async-start(), calls=%async_computation | async-start | bytes 4718592 | tf_op jit(solution)/shard_map/all_gather | solution.py:38
  10.2 182.5 %all-gather.6.cloned.1.call-start = ((), (), s32[]{:S(2)}) async-start(), calls=%async_computation.1 | async-start | bytes 20971520 | tf_op jit(solution)/shard_map/all_gather | solution.py:35
  10.9 309.5 %all-gather.8.cloned.1.call-start = ((), (), s32[]{:S(2)}) async-start(), calls=%async_computation.2 | async-start | bytes 9437184 | tf_op jit(solution)/shard_map/all_gather | solution.py:43
  12.3 1.2 copy-start.3
  14.7 189.5 %copy-start.1 = (bf16[1024,256]{1,0:T(8,128)(2,1)S(1)}, bf16[1024,256]{1,0:T(8,128)(2,1)}, u32[]{:S(2)}) copy-start(bf16[1024,256]{1,0:T(8,128)(2,1)} %broadcast_multiply_fusion) | copy-start | bytes 1572868
  14.8 395.4 %all-reduce.3.cloned.1.call-start = ((), (), s32[]{:S(2)}) async-start(), calls=%async_computation.3 | async-start | bytes 1310720 | tf_op jit(solution)/shard_map/psum | solution.py:62
  320.4 16.3 %copy-start.2 = (bf16[1024,512]{0,1:T(8,128)(2,1)S(1)}, bf16[1024,512]{0,1:T(8,128)(2,1)}, u32[]{:S(2)}) copy-start(bf16[1024,512]{0,1:T(8,128)(2,1)} %convert_multiply_fusion) | copy-start | bytes 3145732
  335.6 1.0 copy-start.7
  335.6 74.5 %copy-start.9 = (f32[1,256,256]{2,1,0:T(8,128)S(1)}, f32[1,256,256]{2,1,0:T(8,128)}, u32[]{:S(2)}) copy-start(f32[1,256,256]{2,1,0:T(8,128)} %param.12) | copy-start | bytes 786436
  335.6 76.9 %copy-start.8 = (f32[2,256,256]{2,1,0:T(8,128)S(1)}, f32[2,256,256]{2,1,0:T(8,128)}, u32[]{:S(2)}) copy-start(f32[2,256,256]{2,1,0:T(8,128)} %param.13) | copy-start | bytes 1572868
  411.1 3.9 copy-start.5
  412.5 2.4 copy-start.4
Sparse Core Ops, SparseCore 0:
  10.7 76.0 all-gather.3
  88.4 104.1 all-gather.5
  195.4 124.9 all-gather.7
  337.9 72.1 all-reduce.2
where the time goes:
time: 422 us
  waiting for transfers between devices  358 us (85%)
  matrix products  37.2 us (9%)
  between operations  13.9 us (3%)
  local copies, waits for them, and re-layouts  6.89 us (2%)
  other arithmetic  4.93 us (1%)
    all_gather x1, waiting for transfers between devices, on_device(): lax.all_gather(low_kid, 'prow', axis=0, tiled=True)  111 us
    all_gather x1, waiting for transfers between devices, on_device(): sigma_rows = lax.all_gather(sigma_top, 'pcol', axis=1, tiled=True)  106 us
    all_gather x1, waiting for transfers between devices, on_device(): lax.all_gather(low_par, 'prow', axis=0, tiled=True)  72.1 us
    psum x1, waiting for transfers between devices, on_device(): lax.psum(part_par.astype(jnp.bfloat16), 'prow').astype(jnp.float32)  69 us
    dot_general x1, matrix products, on_device(): jnp.dot(sigma_rows, lax.all_gather(low_kid, 'prow', axis=0, tiled=True),...  15.2 us
    dot_general x1, matrix products, on_device(): jnp.dot(sigma_rows, lax.all_gather(low_par, 'prow', axis=0, tiled=True),...  11.6 us
  transfers between devices with their start and end apart: 4, of which 4 were waited for; matrix products, arithmetic and copies ran while one was open for 6% of the time, Pallas kernels for 0%

commit v1 on v0

--- a/solution.py
+++ b/solution.py
@@ -1,9 +1,41 @@
+import functools
 import jax
 import jax.numpy as jnp
 from jax import lax
 from jax.sharding import PartitionSpec as P
 
 KIDS = 2
+
+
+def _see_files(x_part, along_dim):
+    big = list(x_part.shape[1:])
+    big[along_dim] *= x_part.shape[0]
+    h_now = jnp.moveaxis(x_part, 0, along_dim).reshape(big)
+    return h_now
+
+
+def works_register(sheet, shard_axis, on_dim):
+    dev_n = lax.axis_size(shard_axis)
+    in_order = list(map(lambda u: (u, (u + 1) % dev_n), range(dev_n)))
+    frames = [(jj, q) for q, jj in in_order]
+    state_next, spare = ([], [])
+    for it in range(dev_n - 1):
+        if it % 2 == 0:
+            state_next.append(
+                lax.ppermute(state_next[-1] if state_next else sheet, shard_axis, in_order)
+            )
+        else:
+            spare.append(
+                lax.ppermute(spare[-1] if spare else sheet, axis_name=shard_axis, perm=frames)
+            )
+    q_next = jnp.stack([*state_next[::-1], sheet, *spare], axis=0)
+    taken_in = lax.axis_index(shard_axis) - len(state_next)
+    q_next = q_next[(jnp.arange(dev_n) - taken_in) % dev_n]
+    item_now = _see_files(q_next, on_dim)
+    return item_now
+
+
+guide_the_edge = functools.partial(works_register, shard_axis="prow", on_dim=0)
 
 
 def expand_rows(mask, width):
@@ -33,11 +65,7 @@
     low_par = panel_par * par_rows.astype(jnp.bfloat16)
     low_kid = panel_kid * kid_rows.astype(jnp.bfloat16)
     sigma_rows = lax.all_gather(sigma_top, "pcol", axis=1, tiled=True)
-    prod_par = jnp.dot(
-        sigma_rows,
-        lax.all_gather(low_par, "prow", axis=0, tiled=True),
-        preferred_element_type=jnp.float32,
-    )
+    prod_par = jnp.dot(sigma_rows, guide_the_edge(low_par), preferred_element_type=jnp.float32)
     prod_kid = jnp.dot(
         sigma_rows,
         lax.all_gather(low_kid, "prow", axis=0, tiled=True),

time: 422 us -> 348 us (0.82)
  waiting for transfers between devices: 358 us -> 230 us
  starting transfers between devices: 0.16 us -> 38.7 us
  local copies, waits for them, and re-layouts: 6.89 us -> 23.3 us
    all_gather x1, waiting for transfers between devices: 106 us -> 0.01 us  [on_device(): sigma_rows = lax.all_gather(sigma_top, 'pcol', axis=1, tiled=True)]
    all_gather x1 -> x0, waiting for transfers between devices: 72.1 us -> none  [on_device(): lax.all_gather(low_par, 'prow', axis=0, tiled=True)]
    ppermute x0 -> x7, waiting for transfers between devices: none -> 49.6 us  [the longest x4 49.6 us: works_register(): lax.ppermute(state_next[-1] if state_next else sheet, shard_axis, in_order)]
    ppermute x0 -> x7, starting transfers between devices: none -> 38.6 us  [the longest x3 30.6 us: works_register(): lax.ppermute(spare[-1] if spare else sheet, axis_name=shard_axis, perm=fr...]
    unnamed x30 -> x38, local copies, waits for them, and re-layouts: 6.55 us -> 17.1 us
    gather x0 -> x1, local copies, waits for them, and re-layouts: none -> 4.98 us  [works_register(): q_next = q_next[(jnp.arange(dev_n) - taken_in) % dev_n]]
  transfers between devices with their start and end apart: 4 -> 10, of which waited for: 4 -> 6; matrix products, arithmetic and copies ran while one was open for 6% -> 12% of each run, Pallas kernels for 0% -> 0%
where the time goes in v1:
time: 348 us; the launch traced here: 347 us
  waiting for transfers between devices  230 us (66%)
  starting transfers between devices  38.7 us (11%)
  matrix products  37.2 us (11%)
  local copies, waits for them, and re-layouts  23.3 us (7%)
  between operations  13.9 us (4%)
  other arithmetic  4.32 us (1%)
    all_gather x1, waiting for transfers between devices, on_device(): lax.all_gather(low_kid, 'prow', axis=0, tiled=True)  110 us
    psum x1, waiting for transfers between devices, on_device(): lax.psum(part_par.astype(jnp.bfloat16), 'prow').astype(jnp.float32)  69 us
    ppermute x4, waiting for transfers between devices, works_register(): lax.ppermute(state_next[-1] if state_next else sheet, shard_axis, in_order)  49.6 us
    ppermute x3, starting transfers between devices, works_register(): lax.ppermute(spare[-1] if spare else sheet, axis_name=shard_axis, perm=fr...  30.6 us
    unnamed x38, local copies, waits for them, and re-layouts  17.1 us
    dot_general x1, matrix products, on_device(): jnp.dot(sigma_rows, lax.all_gather(low_kid, 'prow', axis=0, tiled=True),...  15.2 us
    dot_general x1, matrix products, on_device(): jnp.dot(sigma_rows, guide_the_edge(low_par), preferred_element_type=jnp.f...  11.6 us
    ppermute x4, starting transfers between devices, works_register(): lax.ppermute(state_next[-1] if state_next else sheet, shard_axis, in_order)  8.06 us
  transfers between devices with their start and end apart: 10, of which 6 were waited for; matrix products, arithmetic and copies ran while one was open for 12% of the time, Pallas kernels for 0%

profile of v1, /device:TPU:0, one launch (start us, length us, event | category | flops | bytes accessed | tf_op | source)
XLA Modules:
  0.0 347.1 jit_solution(13108362830967558140)
XLA Ops:
  7.2 0.0 copy-start
  7.2 0.0 all-gather.3.cloned.1.call-start
  7.3 0.7 all-gather.3.cloned.1.call-update
  7.9 0.0 all-gather.5.cloned.1.call-start
  8.0 0.5 copy-done.5
  8.4 0.5 copy.13
  9.0 0.3 broadcast_in_dim.26
  9.4 0.5 copy.29
  9.8 1.1 convert_multiply_fusion
  10.9 0.0 all-gather.5.cloned.1.call-update
  11.0 0.0 all-reduce.3.cloned.1.call-start
  11.0 0.1 broadcast_bitcast_fusion
  11.1 1.2 broadcast_multiply_fusion
  12.4 3.0 collective-permute-start
  15.4 15.0 %collective-permute-done = bf16[1024,256]{1,0:T(8,128)(2,1)S(1)} collective-permute-done((bf16[1024,256]{1,0:T(8,128)(2,1)S(1)}, bf16[1024,256]{1,0:T(8,128)(2,1)S(1)}, u32[]{:S(2)}, u32[]{:S(2)}) %collective-permute-start) | collective-permute-done | bytes 524320 | tf_op jit(solution)/shard_map/ppermute | solution.py:25
  30.3 4.7 %collective-permute-start.4 = (bf16[1024,256]{1,0:T(8,128)(2,1)S(1)}, bf16[1024,256]{1,0:T(8,128)(2,1)}, u32[]{:S(2)}, u32[]{:S(2)}) collective-permute-start(bf16[1024,256]{1,0:T(8,128)(2,1)S(1)} %broadcast_multiply_fusion), channel_id=1, source_target_pairs={{4,0},{8,4},{12,8},{16,12},{20,16},{24,20},{28,24},{0,28},{5,1},{9... | collective-permute-start | bytes 1572872 | tf_op jit(solution)/shard_map/ppermute | solution.py:29
  35.0 17.4 %collective-permute-done.1 = bf16[1024,256]{1,0:T(8,128)(2,1)S(1)} collective-permute-done((bf16[1024,256]{1,0:T(8,128)(2,1)S(1)}, bf16[1024,256]{1,0:T(8,128)(2,1)S(1)}, u32[]{:S(2)}, u32[]{:S(2)}) %collective-permute-start.1) | collective-permute-done | bytes 524320 | tf_op jit(solution)/shard_map/ppermute | solution.py:25
  52.5 2.5 collective-permute-start.2
  55.0 12.2 %collective-permute-start.5 = (bf16[1024,256]{1,0:T(8,128)(2,1)}, bf16[1024,256]{1,0:T(8,128)(2,1)}, u32[]{:S(2)}, u32[]{:S(2)}) collective-permute-start(bf16[1024,256]{1,0:T(8,128)(2,1)} %collective-permute-done.4), channel_id=1, source_target_pairs={{4,0},{8,4},{12,8},{16,12},{20,16},{24,20},{28,24},{0,28},{5,1},{9... | collective-permute-start | bytes 1572872 | tf_op jit(solution)/shard_map/ppermute | solution.py:29
  67.2 9.3 %collective-permute-done.2 = bf16[1024,256]{1,0:T(8,128)(2,1)} collective-permute-done((bf16[1024,256]{1,0:T(8,128)(2,1)S(1)}, bf16[1024,256]{1,0:T(8,128)(2,1)}, u32[]{:S(2)}, u32[]{:S(2)}) %collective-permute-start.2) | collective-permute-done | bytes 524320 | tf_op jit(solution)/shard_map/ppermute | solution.py:25
  76.4 2.6 collective-permute-start.3
  79.0 13.6 %collective-permute-start.6 = (bf16[1024,256]{1,0:T(8,128)(2,1)}, bf16[1024,256]{1,0:T(8,128)(2,1)S(1)}, u32[]{:S(2)}, u32[]{:S(2)}) collective-permute-start(bf16[1024,256]{1,0:T(8,128)(2,1)} %collective-permute-done.5), channel_id=1, source_target_pairs={{4,0},{8,4},{12,8},{16,12},{20,16},{24,20},{28,24},{0,28},{5,1},{9... | collective-permute-start | bytes 1572872 | tf_op jit(solution)/shard_map/ppermute | solution.py:29
  92.7 8.0 %collective-permute-done.3 = bf16[1024,256]{1,0:T(8,128)(2,1)} collective-permute-done((bf16[1024,256]{1,0:T(8,128)(2,1)}, bf16[1024,256]{1,0:T(8,128)(2,1)}, u32[]{:S(2)}, u32[]{:S(2)}) %collective-permute-start.3) | collective-permute-done | bytes 524320 | tf_op jit(solution)/shard_map/ppermute | solution.py:25
  100.7 1.9 bitcast_dynamic-update-slice_fusion.7
  102.6 1.9 bitcast_dynamic-update-slice_fusion.6
  104.5 1.9 bitcast_dynamic-update-slice_fusion.5
  106.4 1.9 bitcast_dynamic-update-slice_fusion.4
  108.3 1.0 bitcast_dynamic-update-slice_fusion.3
  109.3 1.9 bitcast_dynamic-update-slice_fusion.2
  111.1 1.9 bitcast_dynamic-update-slice_fusion.1
  113.0 0.8 bitcast_dynamic-update-slice_fusion
  113.9 5.0 %gather_fusion = bf16[8,1024,256]{2,1,0:T(8,128)(2,1)} fusion(bf16[8,1024,256]{2,1,0:T(8,128)(2,1)} %bitcast_dynamic-update-slice_fusion, s32[1024]{0:T(1024)S(1)} %pad_clamp_fusion), kind=kCustom, calls=%fused_computation | custom fusion | bytes 8388640 | tf_op jit(solution)/shard_map/gather | solution.py:33
  118.8 11.6 %fusion.4 = bf16[256,1024]{1,0:T(8,128)(2,1)S(1)} fusion(bf16[8192,256]{1,0:T(8,128)(2,1)} %bitcast.72, bf16[1024,8192]{1,0:T(8,128)(2,1)} %all-gather.3.cloned.1.call-done, f32[1024]{0:T(1024)S(1)} %bitcast.78), kind=kOutput, calls=%fused_computation.7 | convolution fusion | flops 4295753728 | bytes 21499904 | tf_op jit(solution)/shard_map/dot_general | solution.py:68
  130.4 1.0 fusion.7
  131.5 2.4 convolution_convert_fusion.1
  133.9 1.9 fusion.9
  135.7 110.2 %all-gather.5.cloned.1.call-done = bf16[8192,512]{0,1:T(8,128)(2,1)} async-done(((bf16[1024,512]{0,1:T(8,128)(2,1)}), bf16[8192,512]{0,1:T(8,128)(2,1)}) %all-gather.5.cloned.1.call-update) | async-done | bytes 8388624 | tf_op jit(solution)/shard_map/all_gather | solution.py:71
  246.0 15.2 %fusion.2 = bf16[1024,512]{0,1:T(8,128)(2,1)S(1)} fusion(f32[1024,512]{0,1:T(8,128)S(1)} %bitcast.67, f32[2,1024,256]{1,2,0:T(8,128)} %fusion.9, bf16[8192,512]{0,1:T(8,128)(2,1)} %all-gather.5.cloned.1.call-done, bf16[1024,8192]{1,0:T(8,128)(2,1)} %all-gather.3.cloned.1.call-done), kind=kOutput, calls=%fused_computation.4 | convolution fusion | flops 8592031744 | bytes 30408704 | tf_op jit(solution)/shard_map/dot_general | solution.py:69
  261.3 1.0 copy-done.6
  262.2 1.2 convolution_convert_fusion
  263.4 0.0 all-reduce.3.cloned.1.call-update
  263.4 1.0 copy.20
  264.4 2.3 copy.21
  266.7 69.0 %all-reduce.3.cloned.1.call-done = (bf16[1,256,256]{2,1,0:T(8,128)(2,1)}, bf16[2,256,256]{2,1,0:T(8,128)(2,1)}, bf16[2,256,256]{2,1,0:T(8,128)(2,1)}) async-done(((bf16[1,256,256]{2,1,0:T(8,128)(2,1)}, bf16[2,256,256]{2,1,0:T(8,128)(2,1)}, bf16[2,256,256]{2,1,0:T(8,128)(2,1)}), (bf16[1,256,256]{2,1,0:T(8,128)(2,1)}, bf16[2,256,256]{2,1,0:T(8,128)(2,1)}, ...) | async-done | bytes 655376 | tf_op jit(solution)/shard_map/psum | solution.py:90
  335.7 0.9 convert_subtract_fusion
  336.7 0.0 copy-start.4
  336.7 1.5 fusion.6
  338.2 2.4 fusion.5
  (33 shorter events, 0.1 us)
Async XLA Ops:
  7.2 126.7 %copy-start = (bf16[2,256,256]{2,1,0:T(8,128)(2,1)S(1)}, bf16[2,256,256]{2,1,0:T(8,128)(2,1)}, u32[]{:S(2)}) copy-start(bf16[2,256,256]{2,1,0:T(8,128)(2,1)} %param.11) | copy-start | bytes 786436
  7.2 1.3 copy-start.5
  7.2 1.8 copy-start.11
  7.2 1.8 copy-start.12
  7.2 111.6 %all-gather.3.cloned.1.call-start = ((), (), s32[]{:S(2)}) async-start(), calls=%async_computation | async-start | bytes 20971520 | tf_op jit(solution)/shard_map/all_gather | solution.py:67
  7.9 238.0 %all-gather.5.cloned.1.call-start = ((), (), s32[]{:S(2)}) async-start(), calls=%async_computation.1 | async-start | bytes 9437184 | tf_op jit(solution)/shard_map/all_gather | solution.py:71
  10.9 97.3 %copy-start.2 = (bf16[1024,256]{1,0:T(8,128)(2,1)S(1)}, bf16[1024,256]{1,0:T(8,128)(2,1)}, u32[]{:S(2)}) copy-start(bf16[1024,256]{1,0:T(8,128)(2,1)} %param.9) | copy-start | bytes 1572868
  11.0 324.8 %all-reduce.3.cloned.1.call-start = ((), (), s32[]{:S(2)}) async-start(), calls=%async_computation.2 | async-start | bytes 1310720 | tf_op jit(solution)/shard_map/psum | solution.py:90
  12.4 18.0 %collective-permute-start = (bf16[1024,256]{1,0:T(8,128)(2,1)S(1)}, bf16[1024,256]{1,0:T(8,128)(2,1)S(1)}, u32[]{:S(2)}, u32[]{:S(2)}) collective-permute-start(bf16[1024,256]{1,0:T(8,128)(2,1)S(1)} %broadcast_multiply_fusion), channel_id=1, source_target_pairs={{0,4},{4,8},{8,12},{12,16},{16,20},{20,24},{24,28},{28,0},{1,5},{5... | collective-permute-start | bytes 1572872 | tf_op jit(solution)/shard_map/ppermute | solution.py:25
  30.3 24.6 %copy-start.7 = (bf16[1024,256]{1,0:T(8,128)(2,1)}, bf16[1024,256]{1,0:T(8,128)(2,1)S(1)}, u32[]{:S(2)}) copy-start(bf16[1024,256]{1,0:T(8,128)(2,1)S(1)} %collective-permute-done) | copy-start | bytes 1572868
  30.3 22.1 %collective-permute-start.1 = (bf16[1024,256]{1,0:T(8,128)(2,1)S(1)}, bf16[1024,256]{1,0:T(8,128)(2,1)S(1)}, u32[]{:S(2)}, u32[]{:S(2)}) collective-permute-start(bf16[1024,256]{1,0:T(8,128)(2,1)S(1)} %collective-permute-done), channel_id=1, source_target_pairs={{0,4},{4,8},{8,12},{12,16},{16,20},{20,24},{24,28},{28,0},{1,5},{5... | collective-permute-start | bytes 1572872 | tf_op jit(solution)/shard_map/ppermute | solution.py:25
  30.3 24.6 %collective-permute-start.4 = (bf16[1024,256]{1,0:T(8,128)(2,1)S(1)}, bf16[1024,256]{1,0:T(8,128)(2,1)}, u32[]{:S(2)}, u32[]{:S(2)}) collective-permute-start(bf16[1024,256]{1,0:T(8,128)(2,1)S(1)} %broadcast_multiply_fusion), channel_id=1, source_target_pairs={{4,0},{8,4},{12,8},{16,12},{20,16},{24,20},{28,24},{0,28},{5,1},{9... | collective-permute-start | bytes 1572872 | tf_op jit(solution)/shard_map/ppermute | solution.py:29
  52.5 14.7 %copy-start.8 = (bf16[1024,256]{1,0:T(8,128)(2,1)}, bf16[1024,256]{1,0:T(8,128)(2,1)S(1)}, u32[]{:S(2)}) copy-start(bf16[1024,256]{1,0:T(8,128)(2,1)S(1)} %collective-permute-done.1) | copy-start | bytes 1572868
  52.5 24.0 %collective-permute-start.2 = (bf16[1024,256]{1,0:T(8,128)(2,1)S(1)}, bf16[1024,256]{1,0:T(8,128)(2,1)}, u32[]{:S(2)}, u32[]{:S(2)}) collective-permute-start(bf16[1024,256]{1,0:T(8,128)(2,1)S(1)} %collective-permute-done.1), channel_id=1, source_target_pairs={{0,4},{4,8},{8,12},{12,16},{16,20},{20,24},{24,28},{28,0},{1,5},{5... | collective-permute-start | bytes 1572872 | tf_op jit(solution)/shard_map/ppermute | solution.py:25
  55.0 24.1 %collective-permute-start.5 = (bf16[1024,256]{1,0:T(8,128)(2,1)}, bf16[1024,256]{1,0:T(8,128)(2,1)}, u32[]{:S(2)}, u32[]{:S(2)}) collective-permute-start(bf16[1024,256]{1,0:T(8,128)(2,1)} %collective-permute-done.4), channel_id=1, source_target_pairs={{4,0},{8,4},{12,8},{16,12},{20,16},{24,20},{28,24},{0,28},{5,1},{9... | collective-permute-start | bytes 1572872 | tf_op jit(solution)/shard_map/ppermute | solution.py:29
  76.4 24.3 %collective-permute-start.3 = (bf16[1024,256]{1,0:T(8,128)(2,1)}, bf16[1024,256]{1,0:T(8,128)(2,1)}, u32[]{:S(2)}, u32[]{:S(2)}) collective-permute-start(bf16[1024,256]{1,0:T(8,128)(2,1)} %collective-permute-done.2), channel_id=1, source_target_pairs={{0,4},{4,8},{8,12},{12,16},{16,20},{20,24},{24,28},{28,0},{1,5},{5... | collective-permute-start | bytes 1572872 | tf_op jit(solution)/shard_map/ppermute | solution.py:25
  79.0 34.0 %collective-permute-start.6 = (bf16[1024,256]{1,0:T(8,128)(2,1)}, bf16[1024,256]{1,0:T(8,128)(2,1)S(1)}, u32[]{:S(2)}, u32[]{:S(2)}) collective-permute-start(bf16[1024,256]{1,0:T(8,128)(2,1)} %collective-permute-done.5), channel_id=1, source_target_pairs={{4,0},{8,4},{12,8},{16,12},{20,16},{24,20},{28,24},{0,28},{5,1},{9... | collective-permute-start | bytes 1572872 | tf_op jit(solution)/shard_map/ppermute | solution.py:29
  246.0 16.3 %copy-start.1 = (bf16[1024,512]{0,1:T(8,128)(2,1)S(1)}, bf16[1024,512]{0,1:T(8,128)(2,1)}, u32[]{:S(2)}) copy-start(bf16[1024,512]{0,1:T(8,128)(2,1)} %convert_multiply_fusion) | copy-start | bytes 3145732
  261.2 1.0 copy-start.6
  261.2 74.5 %copy-start.10 = (f32[1,256,256]{2,1,0:T(8,128)S(1)}, f32[1,256,256]{2,1,0:T(8,128)}, u32[]{:S(2)}) copy-start(f32[1,256,256]{2,1,0:T(8,128)} %param.12) | copy-start | bytes 786436
  261.2 76.9 %copy-start.9 = (f32[2,256,256]{2,1,0:T(8,128)S(1)}, f32[2,256,256]{2,1,0:T(8,128)}, u32[]{:S(2)}) copy-start(f32[2,256,256]{2,1,0:T(8,128)} %param.13) | copy-start | bytes 1572868
  336.7 3.9 %copy-start.4 = (f32[1,256,256]{2,1,0:T(8,128)}, f32[1,256,256]{2,1,0:T(8,128)S(1)}, u32[]{:S(2)}) copy-start(f32[1,256,256]{2,1,0:T(8,128)S(1)} %convert_subtract_fusion) | copy-start | bytes 786436
  338.2 2.4 copy-start.3
Sparse Core Ops, SparseCore 0:
  9.6 108.6 all-gather.2
  121.0 124.8 all-gather.4
  263.6 72.1 all-reduce.2
